TPU v7x, 32 devices: a whole 2x2x4 slice. The times are simulated.
32 devices in a mesh: groups: 2 (over x), seq: 16 (over z, y, core).
Axes of the slice: x: 2, y: 2, z: 4, core: 2. Of those that a mesh axis runs over, the one named last changes fastest.
Arguments:
- x_rows: bfloat16 [4096, 4096], P(('groups', 'seq')), parts along dimension 0, may hold values from -6 to 6
- bc_rows: bfloat16 [4096, 256], P(('groups', 'seq')), parts along dimension 0, may hold values from -6 to 6
- step: bfloat16 [4096, 64], P(('groups', 'seq')), parts along dimension 0, may hold values from 1e-06 to 0.3, as said below
- route: int32 [4096, 1], P(('groups', 'seq')), parts along dimension 0, may hold values from 0 to 15; in each aligned block of 128 rows (0 to 127, 128 to 255, ...) at most 12 rows name the same one
- doc_lengths: int32 [16], P('groups'), parts along dimension 0, may hold values from 1 to 1024, 2048 in all
- conv_weight: float32 [4, 4352], replicated, may hold values from -3 to 3
- conv_bias: float32 [4352], replicated, may hold values from -1.2 to 1.2
- rate: float32 [64], replicated, may hold values from 0.5 to 2
- skip: float32 [64], replicated, may hold values from 0.5 to 1.5
- clip_level: float32 [64], replicated, may hold values from 0.3 to 2
Outputs:
- layer_out: bfloat16 [4096, 4096], P(('groups', 'seq')), parts along dimension 0
There are 2 independent parts, one for each index of `groups`. A program takes and returns all parts, laid end to end along the dimension named above; an argument that names none is the same for every part. Nothing has to cross between parts.
Inputs may be any that keep to these rules, and one draw needn't show every extreme that they name: `step`: Positive. `route`: at most 12 of the rows of one device name the same shard; on some device some shard is named exactly 12 times; every shard is named by some row. `doc_lengths`: the lengths sum to 2048; the largest is exactly half of 2048.
All inputs are finite; a program needn't handle non-finite values.
Results may differ from a plain program's by a relative error of at most 0.0038.
Values may be sent and summed in bfloat16 or wider, within the bound.
A program may use at most 320 MiB of HBM per device.

v0:
```python
import functools

import jax
import jax.numpy as jnp
from jax import lax
from jax.experimental import pallas as pl
from jax.experimental.pallas import tpu as pltpu
from jax.sharding import PartitionSpec as P

F32 = jnp.float32
BF16 = jnp.bfloat16
CHUNK = 128
LANES = 128
PAD = 8


def dot(a, b):
    return jnp.dot(a, b, preferred_element_type=F32)


def dot_nt(a, b):
    return lax.dot_general(a, b, (((1,), (1,)), ((), ())), preferred_element_type=F32)


def dot_tn(a, b):
    return lax.dot_general(a, b, (((0,), (0,)), ((), ())), preferred_element_type=F32)


def find_places(aux_ref, ranks, place_row, place_col, heads):
    rows = ranks.shape[0]
    state2 = aux_ref.shape[2] - LANES
    low = lax.broadcasted_iota(jnp.int32, (LANES, LANES), 0)
    high = lax.broadcasted_iota(jnp.int32, (LANES, LANES), 1)
    earlier = jnp.where(low > high, 1.0, 0.0).astype(BF16)
    before = jnp.where(low < high, 1.0, 0.0).astype(BF16)
    shard = high.astype(F32)
    step = 4

    def named(b):
        target = aux_ref[b, :, state2 : state2 + LANES].astype(F32)[:, heads : heads + 1]
        return jnp.where(target == shard, 1.0, 0.0)

    def count(i, total):
        for j in range(step):
            b = i * step + j
            onehot = named(b)
            ranks[pl.ds(pl.multiple_of(b * LANES, LANES), LANES), :] = dot(earlier, onehot.astype(BF16)) + total
            total = total + jnp.sum(onehot, axis=0, keepdims=True)
        return total

    total = lax.fori_loop(0, rows // LANES // step, count, jnp.zeros((1, LANES), F32))
    total = jnp.broadcast_to(total, (8, LANES))
    coarse = jnp.floor(total * (1.0 / 64.0))
    fine = total - coarse * 64.0
    start = (dot(coarse.astype(BF16), before) * 64.0 + dot(fine.astype(BF16), before))[0:1, :]

    def rank(i, _):
        for j in range(step):
            b = i * step + j
            at = pl.multiple_of(b * LANES, LANES)
            found = named(b) * (ranks[pl.ds(at, LANES), :] + start)
            place = jnp.broadcast_to(jnp.sum(found, axis=1, keepdims=True), (LANES, LANES))
            place_col[pl.ds(at, LANES), :] = place
            place_row[:, pl.ds(at, LANES)] = place.T[0:8, :]
        return 0

    lax.fori_loop(0, rows // LANES // step, rank, 0)


def one_hot_sort(place_row, first, size):
    rows = place_row.shape[1]
    number = lax.broadcasted_iota(jnp.int32, (size, rows), 0).astype(F32)
    hit = place_row[0:1, :] - lax.convert_element_type(first, F32) == number
    return jnp.where(hit, 1.0, 0.0).astype(BF16)


def one_hot_unsort(place_col, first, size):
    rows = place_col.shape[0]
    number = lax.broadcasted_iota(jnp.int32, (size, rows), 1).astype(F32)
    place = place_col[pl.ds(first, size), :]
    hit = jnp.concatenate([place] * (rows // LANES), axis=1) == number
    return jnp.where(hit, 1.0, 0.0).astype(BF16)


def doc_begins(at, starts):
    begin = jnp.zeros((CHUNK, 1), jnp.int32)
    for start in starts:
        begin = jnp.where(at >= start, start, begin)
    return begin


def conv_silu(v, par, at, begin):
    acc = par[4:5, :] + par[0:1, :] * v[PAD:, :]
    for j in range(1, 4):
        keep = jnp.where(at - j >= begin, 1.0, 0.0)
        acc = acc + par[j : j + 1, :] * (v[PAD - j : PAD - j + CHUNK, :] * keep)
    return (acc / (1.0 + jnp.exp(-acc))).astype(BF16)


def shared_chunk(c, starts, ub, ds, bcpar_ref, rate_ref, bcs, ws, ent, tails, carries, owned):
    width = ent.shape[1]
    state_width = bcs.shape[1] // 2
    base = pl.multiple_of(c * CHUNK, CHUNK)
    at = lax.broadcasted_iota(jnp.int32, (CHUNK, 1), 0) + base
    begin = doc_begins(at, starts)
    begin_last = begin[CHUNK - 1 :, :]
    act = conv_silu(ub[pl.ds(base, CHUNK + PAD), :], bcpar_ref[...], at, begin)
    bcs[pl.ds(base, CHUNK), :] = act
    b_mat, c_mat = act[:, :state_width], act[:, state_width:]

    dt = ds[pl.ds(base, CHUNK), :]
    low = lax.broadcasted_iota(jnp.int32, (CHUNK, CHUNK), 0)
    high = lax.broadcasted_iota(jnp.int32, (CHUNK, CHUNK), 1)
    tri = jnp.where(low >= high, 1.0, 0.0).astype(BF16)
    cum = -dot(tri, dt.astype(BF16)) * rate_ref[...]
    shifted = (cum - jnp.log(jnp.maximum(dt, 1e-30))).T
    cum_last = cum[CHUNK - 1 :, :]
    scores = dot_nt(c_mat, b_mat)
    scores = jnp.where((low >= high) & (high + base >= begin), scores, 0.0)
    head = lax.broadcasted_iota(jnp.int32, (1, width), 1) // (width // owned)

    def expand(e):
        out = jnp.broadcast_to(e[:, 0:1], (e.shape[0], width))
        for h in range(1, owned):
            out = jnp.where(head == h, e[:, h : h + 1], out)
        return out

    for h in range(owned):
        decay = jnp.exp(cum[:, h : h + 1] - shifted[h : h + 1, :])
        ws[h, pl.ds(base, CHUNK), :] = (scores * decay).astype(BF16)
    ent[pl.ds(base, CHUNK), :] = expand(jnp.exp(cum) * jnp.where(begin < base, 1.0, 0.0))
    tail = jnp.exp(cum_last - cum) * dt * jnp.where(at >= begin_last, 1.0, 0.0)
    tails[pl.ds(base, CHUNK), :] = expand(tail)
    carry = expand(jnp.exp(cum_last) * jnp.where(begin_last < base, 1.0, 0.0))
    carries[c] = jnp.broadcast_to(carry, (8, width))


def scan_chunk(c, part, parts, starts, ux, xpar_ref, bcs, ws, ent, tails, carries, state, ys, owned):
    size = ux.shape[1]
    lanes = slice(part * size, (part + 1) * size)
    state_width = bcs.shape[1] // 2
    base = pl.multiple_of(c * CHUNK, CHUNK)
    at = lax.broadcasted_iota(jnp.int32, (CHUNK, 1), 0) + base
    begin = doc_begins(at, starts)
    x_mat = conv_silu(ux[pl.ds(base, CHUNK + PAD), :], xpar_ref[:, lanes], at, begin)
    x_wide = x_mat.astype(F32)
    bc = bcs[pl.ds(base, CHUNK), :]
    b_mat, c_mat = bc[:, :state_width], bc[:, state_width:]
    local = owned // parts
    head = lax.broadcasted_iota(jnp.int32, (1, size), 1) // (size // local)
    y = xpar_ref[5:6, lanes] * x_wide
    for h in range(local):
        mine = jnp.where(head == h, x_wide, 0.0).astype(BF16)
        y = y + dot(ws[part * local + h, pl.ds(base, CHUNK), :], mine)
    y = y + dot(c_mat, state[...].astype(BF16)) * ent[pl.ds(base, CHUNK), lanes]
    limit = xpar_ref[6:7, lanes]
    ys[pl.ds(base, CHUNK), :] = jnp.clip(y, -limit, limit).astype(BF16)
    scaled = (x_wide * tails[pl.ds(base, CHUNK), lanes]).astype(BF16)
    state[...] = carries[c][0:1, lanes] * state[...] + dot_tn(b_mat, scaled)


def kernel(
    owned, heads, parts, plane, docs_ref, rates, skips, clips, x_ref, aux_ref, weight_ref, bias_ref, out_ref,
    xpar_ref, bcpar_ref, rate_ref, pick_ref, aux_all, x_all, sent, keys, place_row, place_col, ub, ux, ds, bcs, ws, ent, tails, carries, ys, state,
    sorter, unsorter, gate_send, gate_recv, plane_send, x_send, x_recv, out_send, out_recv,
):
    n, tok = x_all.shape[1:3]
    rows, size = ys.shape
    state2 = bcs.shape[1]
    flat = len(x_ref.shape) == 2
    block = max(tok, min(512, (1 << 20) // rows))
    keep = sorter.shape[0] == rows
    me = lax.axis_index("seq")
    inside = lax.rem(me, plane)

    def remote(source, target, send, recv, peer):
        return pltpu.make_async_remote_copy(
            src_ref=source, dst_ref=target, send_sem=send, recv_sem=recv,
            device_id={"seq": peer}, device_id_type=pl.DeviceIdType.MESH,
        )

    def every(count, do, first=0):
        def turn(k, _):
            do(k)
            return 0

        lax.fori_loop(first, count, turn, 0)

    def tile(ref, part, owner):
        if flat:
            return ref.at[:, pl.ds(pl.multiple_of((owner * parts + part) * size, size), size)]
        return ref.at[owner]

    def own_lanes(ref):
        width = size * parts
        if width % LANES == 0:
            return ref[:, pl.ds(pl.multiple_of(me * width, LANES), width)]
        per = LANES // width
        wide = ref[:, pl.ds(pl.multiple_of(me // per * LANES, LANES), LANES)]
        picked = wide[:, :width]
        for i in range(1, per):
            picked = jnp.where(lax.rem(me, per) == i, wide[:, i * width : (i + 1) * width], picked)
        return picked

    def load_params():
        width = size * parts
        head = lax.broadcasted_iota(jnp.int32, (1, width), 1) // (width // owned)
        lane = lax.broadcasted_iota(jnp.int32, (1, LANES), 1)
        gain = level = jnp.zeros((1, width), F32)
        decay = jnp.zeros((1, LANES), F32)
        for h in range(owned):
            gain = jnp.where(head == h, skips[me * owned + h], gain)
            level = jnp.where(head == h, clips[me * owned + h], level)
            decay = jnp.where(lane == h, rates[me * owned + h], decay)
        xpar_ref[0:4, :] = own_lanes(weight_ref)
        xpar_ref[4:5, :] = own_lanes(bias_ref)
        xpar_ref[5:6, :] = gain
        xpar_ref[6:7, :] = level
        first = weight_ref.shape[1] - state2
        bcpar_ref[0:4, :] = weight_ref[:, first:]
        bcpar_ref[4:5, :] = bias_ref[:, first:]
        rate_ref[...] = decay
        source = lax.broadcasted_iota(jnp.int32, (LANES, LANES), 0)
        target = lax.broadcasted_iota(jnp.int32, (LANES, LANES), 1)
        hit = (source == target + me * owned) & (target < owned)
        pick_ref[...] = jnp.where(hit, 1.0, 0.0).astype(BF16)

    barrier = pltpu.get_barrier_semaphore()

    def greet(k):
        pl.semaphore_signal(
            barrier, inc=1, device_id={"seq": lax.rem(me + k, n)}, device_id_type=pl.DeviceIdType.MESH
        )

    every(n, greet, 1)
    pl.semaphore_wait(barrier, n - 1)

    def far(k):
        peer = lax.rem(me + k * plane, n)
        return remote(aux_ref, aux_all.at[me], gate_send.at[k], gate_recv.at[me], peer)

    def landed(ref, sems, slot):
        return remote(ref.at[slot], ref.at[slot], gate_send.at[0], sems.at[slot], slot)

    across = me - inside + lax.rem(inside + 2, plane)
    sibling = me + 1 - 2 * lax.rem(me, 2)

    def relay(k, hop):
        owner = lax.rem((across if hop == 2 else me) + k * plane, n)
        peer = across if hop == 0 else sibling
        return remote(aux_all.at[owner], aux_all.at[owner], plane_send.at[k, hop], gate_recv.at[owner], peer)

    def x_copy(part, k):
        peer = lax.rem(me + k, n)
        return remote(tile(x_ref, part, peer), x_all.at[part, me], x_send.at[part, k], x_recv.at[part, me], peer)

    every(n // plane, lambda k: far(k).start(), 1)
    aux_all[me] = aux_ref[...]
    relay(0, 0).start()
    relay(0, 1).start()

    def forward(k):
        landed(aux_all, gate_recv, lax.rem(me + k * plane, n)).wait_recv()
        relay(k, 0).start()
        relay(k, 1).start()

    every(n // plane, forward, 1)
    for part in range(parts):
        x_all[part, me] = tile(x_ref, part, me)[...]

    load_params()

    def crossed(k):
        landed(aux_all, gate_recv, lax.rem(across + k * plane, n)).wait_recv()
        relay(k, 2).start()

    every(n // plane, crossed)
    every(n, lambda k: x_copy(0, k).start(), 1)
    for part in range(1, parts):
        every(n, lambda k: x_copy(part, k).start(), 1)

    def rest(k):
        for hop in (0, 2):
            owner = sibling - lax.rem(sibling, plane) + lax.rem(lax.rem(sibling, plane) + hop, plane)
            landed(aux_all, gate_recv, lax.rem(owner + k * plane, n)).wait_recv()

    every(n // plane, rest)
    aux_rows = aux_all
    find_places(aux_rows, keys, place_row, place_col, heads)
    ub[0:PAD, :] = jnp.zeros((PAD, state2), F32)
    ux[0:PAD, :] = jnp.zeros((PAD, size), F32)

    def gather(b):
        first = pl.multiple_of(b * block, block)
        onehot = one_hot_sort(place_row, first, block)
        if keep:
            sorter[pl.ds(first, block), :] = onehot
        aux_here = dot(onehot, aux_all[...].reshape(rows, aux_all.shape[2]))
        ub[pl.ds(pl.multiple_of(first + PAD, PAD), block), :] = aux_here[:, :state2]
        ds[pl.ds(first, block), :] = dot(aux_here[:, state2:].astype(BF16), pick_ref[...])

    every(rows // block, gather)

    starts, total = [], jnp.int32(0)
    for k in range(docs_ref.shape[0]):
        starts.append(total)
        total = total + docs_ref[k]

    def shared(c):
        for i in range(4):
            shared_chunk(4 * c + i, starts, ub, ds, bcpar_ref, rate_ref, bcs, ws, ent, tails, carries, owned)

    every(rows // CHUNK // 4, shared)
    if keep:

        def prepare(b):
            first = pl.multiple_of(b * block, block)
            unsorter[pl.ds(first, block), :] = one_hot_unsort(place_col, first, block)

        every(rows // block, prepare)

    def out_copy(part, owner):
        return remote(
            sent.at[part, owner], tile(out_ref, part, me), out_send.at[part, owner], out_recv.at[part, me], owner
        )

    for part in range(parts):

        def x_landed(k):
            source = lax.rem(me + k, n)
            slot = x_all.at[part, source]
            remote(slot, slot, gate_send.at[0], x_recv.at[part, source], source).wait_recv()

        every(n, x_landed, 1)

        def gather_x(b):
            first = pl.multiple_of(b * block, block)
            onehot = sorter[pl.ds(first, block), :] if keep else one_hot_sort(place_row, first, block)
            x_here = dot(onehot, x_all[part].reshape(rows, size))
            ux[pl.ds(pl.multiple_of(first + PAD, PAD), block), :] = x_here

        every(rows // block, gather_x)
        state[...] = jnp.zeros_like(state)

        def chunk(c):
            for i in range(4):
                scan_chunk(
                    4 * c + i, part, parts, starts, ux, xpar_ref, bcs, ws, ent, tails, carries, state, ys, owned
                )

        every(rows // CHUNK // 4, chunk)

        def scatter(i):
            b = lax.rem(me * tok // block + 1 + i, rows // block)
            first = pl.multiple_of(b * block, block)
            onehot = unsorter[pl.ds(first, block), :] if keep else one_hot_unsort(place_col, first, block)
            back = dot(onehot, ys[...]).astype(BF16)
            for j in range(block // tok):
                owner = b * (block // tok) + j
                sent[part, owner] = back[j * tok : (j + 1) * tok, :]

                @pl.when(owner != me)
                def _():
                    out_copy(part, owner).start()

        every(rows // block, scatter)
        tile(out_ref, part, me)[...] = sent[part, me]

    def finish(k):
        source = lax.rem(me + k, n)
        for part in range(parts):
            slot = tile(out_ref, part, source)
            remote(slot, slot, gate_send.at[0], out_recv.at[part, source], source).wait_recv()
            out_copy(part, source).wait_send()
            x_copy(part, k).wait_send()

    every(n, finish, 1)

    def finish_aux(k):
        for hop in range(3):
            relay(k, hop).wait_send()

    every(n // plane, finish_aux)
    every(n // plane, lambda k: far(k).wait_send(), 1)


def per_device(
    x_rows, bc_rows, step, route, doc_lengths, conv_weight, conv_bias, rate, skip, clip_level
):
    seq_count = lax.axis_size("seq")
    tok_rows, hp_width = x_rows.shape
    heads = step.shape[1]
    owned = heads // seq_count
    width = hp_width // seq_count
    state2 = bc_rows.shape[1]
    rows = tok_rows * seq_count

    spare = jnp.zeros((tok_rows, LANES - heads - 1), BF16)
    aux = jnp.concatenate([bc_rows, step, route.astype(BF16), spare], axis=1)
    parts = 2 if width % (2 * LANES) == 0 and owned % 2 == 0 else 1
    plane = 4
    size = width // parts
    keep = rows if rows <= 2048 else 16
    flat = size % LANES == 0
    x_send = x_rows if flat else jnp.swapaxes(x_rows.reshape(tok_rows, seq_count, width), 0, 1)

    vmem = pl.BlockSpec(memory_space=pltpu.VMEM)
    dma = pltpu.SemaphoreType.DMA
    out = pl.pallas_call(
        functools.partial(kernel, owned, heads, parts, plane),
        out_shape=jax.ShapeDtypeStruct(x_send.shape, BF16),
        in_specs=[pl.BlockSpec(memory_space=pltpu.SMEM)] * 4 + [vmem] * 4,
        out_specs=vmem,
        scratch_shapes=[
            pltpu.VMEM((8, width), F32),
            pltpu.VMEM((8, state2), F32),
            pltpu.VMEM((1, LANES), F32),
            pltpu.VMEM((LANES, LANES), BF16),
            pltpu.VMEM((seq_count, tok_rows, aux.shape[1]), BF16),
            pltpu.VMEM((parts, seq_count, tok_rows, size), BF16),
            pltpu.VMEM((parts, seq_count, tok_rows, size), BF16),
            pltpu.VMEM((rows, LANES), F32),
            pltpu.VMEM((8, rows), F32),
            pltpu.VMEM((rows, LANES), F32),
            pltpu.VMEM((PAD + rows, state2), F32),
            pltpu.VMEM((PAD + rows, size), F32),
            pltpu.VMEM((rows, LANES), F32),
            pltpu.VMEM((rows, state2), BF16),
            pltpu.VMEM((owned, rows, CHUNK), BF16),
            pltpu.VMEM((rows, width), F32),
            pltpu.VMEM((rows, width), F32),
            pltpu.VMEM((rows // CHUNK, 8, width), F32),
            pltpu.VMEM((rows, size), BF16),
            pltpu.VMEM((state2 // 2, size), F32),
            pltpu.VMEM((keep, keep), BF16),
            pltpu.VMEM((keep, keep), BF16),
            dma((seq_count // plane,)),
            dma((seq_count,)),
            dma((seq_count // plane, 3)),
            dma((parts, seq_count)),
            dma((parts, seq_count)),
            dma((parts, seq_count)),
            dma((parts, seq_count)),
        ],
        compiler_params=pltpu.CompilerParams(
            vmem_limit_bytes=60 * 1024 * 1024, collective_id=0, has_side_effects=True
        ),
    )(doc_lengths, rate, skip, clip_level, x_send, aux, conv_weight, conv_bias[None, :])
    return out if flat else jnp.swapaxes(out, 0, 1).reshape(tok_rows, hp_width)


def solution(mesh):
    placed = (
        P(("groups", "seq"), None),
        P(("groups", "seq"), None),
        P(("groups", "seq"), None),
        P(("groups", "seq"), None),
        P("groups"),
        P(),
        P(),
        P(),
        P(),
        P(),
    )
    return jax.shard_map(
        per_device,
        mesh=mesh,
        in_specs=placed,
        out_specs=P(("groups", "seq"), None),
        check_vma=False,
    )
```

profile of v0, /device:TPU:9, one launch (start us, length us, event | category | flops | bytes accessed | tf_op | source)
XLA Modules:
  0.0 79.8 jit_solution(11248679461785417181)
XLA Ops:
  0.0 0.0 copy-start
  0.0 0.7 convert_element_type.3
  0.7 0.1 pad.3.clone
  0.8 1.3 %broadcast_in_dim.7.bias_ref = f32[1,4352]{1,0:T(1,128)} reshape(f32[4352]{0:T(1024)} %param.16) | data formatting | bytes 34816 | tf_op jit(solution)/shard_map/broadcast_in_dim | solution.py:448
  2.1 0.1 copy.12
  2.2 0.8 %copy.11 = bf16[128,64]{1,0:T(8,128)(2,1)S(1)} copy(bf16[128,64]{0,1:T(8,128)(2,1)} %param.12) | data formatting | bytes 32768 | tf_op args[2]
  3.1 0.0 copy-done
  3.1 0.7 maximum_maximum_fusion.aux_ref
  3.8 73.7 %shard_map.100 = bf16[128,4096]{1,0:T(8,128)(2,1)} custom-call(s32[8]{0:T(128)} %docs_ref.1, f32[64]{0:T(128)} %rates.1, f32[64]{0:T(128)} %skips.1, f32[64]{0:T(128)} %clips.1, bf16[128,4096]{1,0:T(8,128)(2,1)} %x_ref.1, bf16[128,384]{1,0:T(8,128)(2,1)} %maximum_maximum_fusion.aux_ref, f32[4,4352]{1,0:T(4,128)} %weight_ref.1, ...), custom_call_target="tpu_custom_call" | custom-call | tf_op jit(solution)/shard_map/pallas_call | solution.py:409
  77.5 2.3 %copy.14 = bf16[128,4096]{1,0:T(8,128)(2,1)} copy(bf16[128,4096]{1,0:T(8,128)(2,1)} %shard_map.100) | data formatting | bytes 2097152
  (1 shorter events, 0.0 us)
Async XLA Ops:
  0.0 3.1 %copy-start = (bf16[128,256]{1,0:T(8,128)(2,1)S(1)}, bf16[128,256]{1,0:T(8,128)(2,1)}, u32[]{:S(2)}) copy-start(bf16[128,256]{1,0:T(8,128)(2,1)} %param.11) | copy-start | bytes 196612
where the time goes:
time: 80.6 us; the launch traced here: 79.8 us
  Pallas kernels  73.7 us (91%)
  local copies, waits for them, and re-layouts  4.67 us (6%)
  other arithmetic  1.42 us (2%)
    pallas_call x1, Pallas kernels, per_device(): pl.pallas_call(functools.partial(kernel, owned, heads, parts, plane), out...  73.7 us
    unnamed x4, local copies, waits for them, and re-layouts  3.12 us

commit v1 on v0

--- a/solution.py
+++ b/solution.py
@@ -12,6 +12,7 @@
 CHUNK = 128
 LANES = 128
 PAD = 8
+OUT_SPEC = pl.BlockSpec(memory_space=pl.ANY)
 
 
 def dot(a, b):
@@ -449,6 +450,473 @@
     return out if flat else jnp.swapaxes(out, 0, 1).reshape(tok_rows, hp_width)
 
 
+SUB = 256
+SMALL = 16
+
+
+def fast_conv(rows, taps, bias, off):
+    size = off.shape[0]
+    acc = bias + taps[0:1, :] * rows[PAD : PAD + size, :]
+    for j in range(1, 4):
+        back = rows[PAD - j : PAD - j + size, :]
+        acc = acc + taps[j : j + 1, :] * jnp.where(off >= j, back, 0.0)
+    half = 0.5 * acc
+    return (half + half * jnp.tanh(half)).astype(BF16)
+
+
+def fast_kernel(
+    owned, parts, plane, docs_ref, rates, skips, clips, x_ref, bc_ref, step_ref, route_ref, weight_ref, bias_ref, out_ref,
+    step_v, route_v, x_taps, bc_taps, bias_v, small_out, small_all, bc_all, x_all, sent, off_ref,
+    sorter, unsorter, dt_left, dt_right, places, ub, ux, lhs, b_flip, rise, fall, by_chunk, ys, state,
+    load_sem, small_send, small_recv, gate_send, gate_recv, plane_send, x_send, x_recv, own_sem, out_send, out_recv,
+):
+    n, tok, state2 = bc_all.shape
+    rows, size = ys.shape
+    heads = step_v.shape[0]
+    chunks = rows // CHUNK
+    width = size * parts
+    local = owned // parts
+    me = lax.axis_index("seq")
+    inside = lax.rem(me, plane)
+    iota = functools.partial(lax.broadcasted_iota, jnp.int32)
+
+    def remote(source, target, send, recv, peer):
+        return pltpu.make_async_remote_copy(
+            src_ref=source, dst_ref=target, send_sem=send, recv_sem=recv,
+            device_id={"seq": peer}, device_id_type=pl.DeviceIdType.MESH,
+        )
+
+    def every(count, do, first=0):
+        def turn(k, _):
+            do(k)
+            return 0
+
+        lax.fori_loop(first, count, turn, 0)
+
+    def tile(ref, part, owner):
+        return ref.at[:, pl.ds(pl.multiple_of((owner * parts + part) * size, size), size)]
+
+    barrier = pltpu.get_barrier_semaphore()
+
+    def greet(k):
+        pl.semaphore_signal(
+            barrier, inc=1, device_id={"seq": lax.rem(me + k, n)}, device_id_type=pl.DeviceIdType.MESH
+        )
+
+    every(n, greet, 1)
+
+    own = pl.ds(pl.multiple_of(me * width, width), width)
+    shared_at = weight_ref.shape[1] - state2
+    loads = [
+        pltpu.make_async_copy(bc_ref, bc_all.at[me], load_sem.at[0]),
+        pltpu.make_async_copy(step_ref, step_v, load_sem.at[1]),
+        pltpu.make_async_copy(route_ref, route_v, load_sem.at[2]),
+        pltpu.make_async_copy(weight_ref.at[:, own], x_taps, load_sem.at[3]),
+        pltpu.make_async_copy(weight_ref.at[:, shared_at:], bc_taps, load_sem.at[4]),
+        pltpu.make_async_copy(bias_ref, bias_v, load_sem.at[5]),
+    ]
+    for load in loads:
+        load.start()
+
+    loads[1].wait()
+    loads[2].wait()
+    wide_step = step_v[...].astype(F32)
+    wide_route = jnp.broadcast_to(route_v[...].astype(F32), (8, tok))
+    for p in range(n):
+        mine = wide_step[p * owned : (p + 1) * owned, :]
+        block = jnp.concatenate([mine, jnp.zeros((8 - owned, tok), F32), wide_route], axis=0)
+        small_out[p] = block.astype(BF16)
+    small_all[me] = small_out[me]
+    loads[0].wait()
+
+    pl.semaphore_wait(barrier, n - 1)
+
+    def far(k):
+        peer = lax.rem(me + k * plane, n)
+        return remote(bc_all.at[me], bc_all.at[me], gate_send.at[k], gate_recv.at[me], peer)
+
+    def small_copy(k):
+        peer = lax.rem(me + k, n)
+        return remote(small_out.at[peer], small_all.at[me], small_send.at[k], small_recv.at[me], peer)
+
+    def landed(ref, sems, slot):
+        return remote(ref.at[slot], ref.at[slot], gate_send.at[0], sems.at[slot], slot)
+
+    across = me - inside + lax.rem(inside + 2, plane)
+    sibling = me + 1 - 2 * lax.rem(me, 2)
+
+    def relay(k, hop):
+        owner = lax.rem((across if hop == 2 else me) + k * plane, n)
+        peer = across if hop == 0 else sibling
+        return remote(bc_all.at[owner], bc_all.at[owner], plane_send.at[k, hop], gate_recv.at[owner], peer)
+
+    def x_copy(part, k):
+        peer = lax.rem(me + k, n)
+        return remote(tile(x_ref, part, peer), x_all.at[part, me], x_send.at[part, k], x_recv.at[part, me], peer)
+
+    def own_copy(part):
+        return pltpu.make_async_copy(tile(x_ref, part, me), x_all.at[part, me], own_sem.at[part])
+
+    every(n, lambda k: small_copy(k).start(), 1)
+    every(n // plane, lambda k: far(k).start(), 1)
+    relay(0, 0).start()
+    relay(0, 1).start()
+    for part in range(parts):
+        own_copy(part).start()
+    for part in range(parts):
+        every(n, lambda k: x_copy(part, k).start(), 1)
+
+    starts, total = [], jnp.int32(0)
+    for k in range(docs_ref.shape[0]):
+        starts.append(total)
+        total = total + docs_ref[k]
+
+    def begins(at):
+        begin = jnp.zeros(at.shape, jnp.int32)
+        for start in starts:
+            begin = jnp.where(at >= start, start, begin)
+        return begin
+
+    def forward(k):
+        landed(bc_all, gate_recv, lax.rem(me + k * plane, n)).wait_recv()
+        relay(k, 0).start()
+        relay(k, 1).start()
+
+    every(n // plane, forward, 1)
+
+    def small_landed(k):
+        landed(small_all, small_recv, lax.rem(me + k, n)).wait_recv()
+
+    every(n, small_landed, 1)
+
+    low, high = iota((CHUNK, CHUNK), 0), iota((CHUNK, CHUNK), 1)
+
+    def find_places():
+        number = iota((n, tok), 0).astype(F32)
+        named = []
+        for i in range(n):
+            target = jnp.concatenate([small_all[i].astype(F32)[8:, :]] * (n // 8), axis=0)
+            named.append(jnp.where(target == number, 1.0, 0.0))
+        earlier = jnp.where(low < high, 1.0, 0.0).astype(BF16)
+        right = jnp.concatenate([earlier, jnp.ones((tok, tok), BF16)], axis=1)
+        found = dot(jnp.concatenate(named, axis=0).astype(BF16), right)
+        before = jnp.zeros((n, tok), F32)
+        ranks = []
+        for i in range(n):
+            here = found[i * n : (i + 1) * n, :]
+            ranks.append(here[:, :tok] + before)
+            before = before + here[:, tok:]
+        base = jnp.zeros((n, tok), F32)
+        for d in range(n - 1):
+            base = base + jnp.where(number > d, before[d : d + 1, :], 0.0)
+        for i in range(n):
+            place = jnp.sum(named[i] * (ranks[i] + base), axis=0, keepdims=True)
+            places[i : i + 1, :] = place
+            coarse = jnp.floor(place * (1.0 / CHUNK))
+            fine = place - coarse * CHUNK
+            lanes = slice(i * tok, (i + 1) * tok)
+            steps = small_all[i].astype(F32)[0:8, :]
+            split = [jnp.where(coarse == c, steps, 0.0) for c in range(chunks)]
+            dt_left[:, lanes] = jnp.concatenate(split, axis=0).astype(BF16)
+            dt_right[:, lanes] = jnp.where(low.astype(F32) == fine, 1.0, 0.0).astype(BF16)
+
+    find_places()
+
+    row16 = iota((SUB, tok), 0).astype(F32).astype(BF16)
+    one, none = jnp.ones((), BF16), jnp.zeros((), BF16)
+
+    def make_sorter(b):
+        first = lax.convert_element_type(b * SUB, F32)
+        for i in range(n):
+            rel = places[i : i + 1, :] - first
+            rel = jnp.where((rel >= 0.0) & (rel < SUB), rel, -1.0)
+            rel = jnp.broadcast_to(rel, (SUB, tok)).astype(BF16)
+            hit = jnp.where(row16 == rel, one, none)
+            sorter[pl.ds(pl.multiple_of(b * SUB, SUB), SUB), i * tok : (i + 1) * tok] = hit
+
+    every(rows // SUB, make_sorter)
+
+    def crossed(k):
+        landed(bc_all, gate_recv, lax.rem(across + k * plane, n)).wait_recv()
+        relay(k, 2).start()
+
+    every(n // plane, crossed)
+
+    def make_off(c):
+        base = pl.multiple_of(c * CHUNK, CHUNK)
+        at = low + base
+        off_ref[pl.ds(base, CHUNK), :] = (at - begins(at)).astype(F32)
+
+    every(chunks, make_off)
+
+    def decays():
+        dts = dot_nt(dt_left[...], dt_right[...])
+        lane = iota((8, CHUNK), 1)
+        slot = iota((8, CHUNK), 0)
+        rate = jnp.zeros((8, CHUNK), F32)
+        for h in range(owned):
+            rate = jnp.where(slot == h, rates[me * owned + h], rate)
+        rate = jnp.concatenate([rate] * chunks, axis=0)
+        upto = jnp.where(low <= high, 1.0, 0.0).astype(BF16)
+        cum = -dot(dts.astype(BF16), upto) * rate
+        last = jnp.broadcast_to(cum[:, CHUNK - 1 :], cum.shape)
+        middle = 0.5 * last
+        up = jnp.exp(cum - middle)
+        down = jnp.exp(middle - cum) * dts
+        gain = jnp.exp(middle)
+        number = iota((8 * chunks, CHUNK), 0) // 8
+        ends = number * CHUNK + CHUNK - 1
+        goes_on = jnp.where(begins(ends) < number * CHUNK, 1.0, 0.0)
+        carry = jnp.exp(last) * goes_on
+        by_chunk[0] = up
+        by_chunk[1] = down
+        by_chunk[2] = gain
+        by_chunk[3] = carry
+
+    decays()
+
+    head = iota((1, size), 1) // (size // local)
+
+    def spread(columns, part):
+        out = jnp.broadcast_to(columns[:, part * local : part * local + 1], (CHUNK, size))
+        for h in range(1, local):
+            at = part * local + h
+            out = jnp.where(head == h, jnp.broadcast_to(columns[:, at : at + 1], (CHUNK, size)), out)
+        return out
+
+    def expand(c):
+        base = pl.multiple_of(c * CHUNK, CHUNK)
+        at8 = pl.ds(pl.multiple_of(c * 8, 8), 8)
+        rest = jnp.zeros((CHUNK - 16, CHUNK), F32)
+        columns = jnp.concatenate([by_chunk[0, at8, :], by_chunk[1, at8, :], rest], axis=0).T
+        for part in range(parts):
+            rise[part, pl.ds(base, CHUNK), :] = spread(columns, part)
+            fall[part, pl.ds(base, CHUNK), :] = spread(columns[:, 8:], part)
+
+    every(chunks // 4, lambda c: [expand(4 * c + i) for i in range(4)])
+
+    def rest(k):
+        for hop in (0, 2):
+            owner = sibling - lax.rem(sibling, plane) + lax.rem(lax.rem(sibling, plane) + hop, plane)
+            landed(bc_all, gate_recv, lax.rem(owner + k * plane, n)).wait_recv()
+
+    every(n // plane, rest)
+
+    for load in loads[3:]:
+        load.wait()
+    ub[0:PAD, :] = jnp.zeros((PAD, state2), F32)
+    ux[0:PAD, :] = jnp.zeros((PAD, size), F32)
+    block = 512
+
+    def gather(b):
+        first = pl.multiple_of(b * block, block)
+        here = dot(sorter[pl.ds(first, block), :], bc_all[...].reshape(rows, state2))
+        ub[pl.ds(pl.multiple_of(first + PAD, PAD), block), :] = here
+
+    every(rows // block, gather)
+
+    gap = low - high
+
+    def wide_bias(first, count):
+        return jnp.concatenate([bias_v[pl.ds(first + i, 1), :] for i in range(count)], axis=1)
+
+    def shared(c):
+        base = pl.multiple_of(c * CHUNK, CHUNK)
+        off = off_ref[pl.ds(base, CHUNK), :]
+        off2 = jnp.concatenate([off] * (state2 // LANES), axis=1)
+        bias = wide_bias(shared_at // LANES, state2 // LANES)
+        act = fast_conv(ub[pl.ds(base, CHUNK + PAD), :], bc_taps[...], bias, off2)
+        b_mat, c_mat = act[:, : state2 // 2], act[:, state2 // 2 :]
+        scores = dot_nt(c_mat, b_mat)
+        keep = (gap >= 0) & (gap.astype(F32) <= off)
+        lhs[pl.ds(base, CHUNK), :CHUNK] = jnp.where(keep, scores, 0.0).astype(BF16)
+        runs_in = jnp.where(off > low.astype(F32), c_mat.astype(F32), 0.0)
+        lhs[pl.ds(base, CHUNK), CHUNK:] = runs_in.astype(BF16)
+        runs_out = high[0:1, :].astype(F32) + off[CHUNK - 1 :, :] >= CHUNK - 1
+        b_flip[pl.ds(base, CHUNK), :] = jnp.where(runs_out, b_mat.astype(F32).T, 0.0).astype(BF16)
+
+    every(chunks // 4, lambda c: [shared(4 * c + i) for i in range(4)])
+
+    col16 = iota((tok, SUB), 1).astype(F32).astype(BF16)
+    flipped = jnp.concatenate([places[...], jnp.zeros((tok - n, tok), F32)], axis=0).T
+
+    def make_unsorter(b):
+        first = lax.convert_element_type(b * SUB, F32)
+        for i in range(n):
+            rel = jnp.broadcast_to(flipped[:, i : i + 1], (tok, tok)) - first
+            rel = jnp.where((rel >= 0.0) & (rel < SUB), rel, -1.0).astype(BF16)
+            hit = jnp.where(col16 == jnp.concatenate([rel] * (SUB // tok), axis=1), one, none)
+            unsorter[i * tok : (i + 1) * tok, pl.ds(pl.multiple_of(b * SUB, SUB), SUB)] = hit
+
+    every(rows // SUB, make_unsorter)
+
+    def out_copy(part, owner):
+        return remote(
+            sent.at[part, owner], tile(out_ref, part, me), out_send.at[part, owner], out_recv.at[part, me], owner
+        )
+
+    def own_out(part):
+        return pltpu.make_async_copy(sent.at[part, me], tile(out_ref, part, me), own_sem.at[parts + part])
+
+    lane_head = iota((1, size), 1) // (size // local)
+
+    def by_head(values):
+        out = jnp.full((1, size), values[0], F32)
+        for h in range(1, local):
+            out = jnp.where(lane_head == h, values[h], out)
+        return out
+
+    for part in range(parts):
+
+        def x_landed(k):
+            source = lax.rem(me + k, n)
+            slot = x_all.at[part, source]
+            remote(slot, slot, gate_send.at[0], x_recv.at[part, source], source).wait_recv()
+
+        own_copy(part).wait()
+        every(n, x_landed, 1)
+
+        def gather_x(b):
+            first = pl.multiple_of(b * block, block)
+            here = dot(sorter[pl.ds(first, block), :], x_all[part].reshape(rows, size))
+            ux[pl.ds(pl.multiple_of(first + PAD, PAD), block), :] = here
+
+        every(rows // block, gather_x)
+        state[...] = jnp.zeros_like(state)
+        skip = by_head([skips[me * owned + part * local + h] for h in range(local)])
+        level = by_head([clips[me * owned + part * local + h] for h in range(local)])
+
+        def chunk(c):
+            base = pl.multiple_of(c * CHUNK, CHUNK)
+            at = pl.ds(base, CHUNK)
+            bias = bias_v[pl.ds(me * parts + part, 1), :]
+            taps = x_taps[:, part * size : (part + 1) * size]
+            wide = fast_conv(ux[pl.ds(base, CHUNK + PAD), :], taps, bias, off_ref[at, :]).astype(F32)
+            scaled = (wide * fall[part, at, :]).astype(BF16)
+            at8 = pl.ds(pl.multiple_of(c * 8, 8), 8)
+            gains, carries = by_chunk[2, at8, :], by_chunk[3, at8, :]
+            gain = by_head([gains[part * local + h : part * local + h + 1, :] for h in range(local)])
+            carry = by_head([carries[part * local + h : part * local + h + 1, :] for h in range(local)])
+            old = state[...]
+            right = jnp.concatenate([scaled, (gain * old).astype(BF16)], axis=0)
+            y = skip * wide + rise[part, at, :] * dot(lhs[at, :], right)
+            ys[at, :] = jnp.clip(y, -level, level).astype(BF16)
+            state[...] = carry * old + gain * dot(b_flip[at, :], scaled)
+
+        every(chunks // 4, lambda c: [chunk(4 * c + i) for i in range(4)])
+
+        def scatter(i):
+            b = lax.rem(me * tok // block + 1 + i, rows // block)
+            first = pl.multiple_of(b * block, block)
+            back = dot(unsorter[pl.ds(first, block), :], ys[...]).astype(BF16)
+            for j in range(block // tok):
+                owner = b * (block // tok) + j
+                sent[part, owner] = back[j * tok : (j + 1) * tok, :]
+
+                @pl.when(owner != me)
+                def _():
+                    out_copy(part, owner).start()
+
+        every(rows // block, scatter)
+        own_out(part).start()
+
+    def finish(k):
+        source = lax.rem(me + k, n)
+        for part in range(parts):
+            slot = tile(out_ref, part, source)
+            remote(slot, slot, gate_send.at[0], out_recv.at[part, source], source).wait_recv()
+            out_copy(part, source).wait_send()
+            x_copy(part, k).wait_send()
+        small_copy(k).wait_send()
+
+    every(n, finish, 1)
+    for part in range(parts):
+        own_out(part).wait()
+
+    def finish_aux(k):
+        for hop in range(3):
+            relay(k, hop).wait_send()
+
+    every(n // plane, finish_aux)
+    every(n // plane, lambda k: far(k).wait_send(), 1)
+
+
+def fast_device(
+    x_rows, bc_rows, step, route, doc_lengths, conv_weight, conv_bias, rate, skip, clip_level
+):
+    n = lax.axis_size("seq")
+    tok, hp_width = x_rows.shape
+    heads = step.shape[1]
+    owned = heads // n
+    width = hp_width // n
+    state2 = bc_rows.shape[1]
+    rows = tok * n
+    parts = width // LANES
+    size = LANES
+    plane = 4
+    chunks = rows // CHUNK
+    bias = conv_bias.reshape(conv_bias.shape[0] // LANES, LANES)
+
+    hbm = pl.BlockSpec(memory_space=pl.ANY)
+    dma = pltpu.SemaphoreType.DMA
+    return pl.pallas_call(
+        functools.partial(fast_kernel, owned, parts, plane),
+        out_shape=jax.ShapeDtypeStruct(x_rows.shape, BF16),
+        in_specs=[pl.BlockSpec(memory_space=pltpu.SMEM)] * 4 + [hbm] * 6,
+        out_specs=OUT_SPEC,
+        scratch_shapes=[
+            pltpu.VMEM((heads, tok), BF16),
+            pltpu.VMEM((1, tok), jnp.int32),
+            pltpu.VMEM((4, width), F32),
+            pltpu.VMEM((4, state2), F32),
+            pltpu.VMEM(bias.shape, F32),
+            pltpu.VMEM((n, SMALL, tok), BF16),
+            pltpu.VMEM((n, SMALL, tok), BF16),
+            pltpu.VMEM((n, tok, state2), BF16),
+            pltpu.VMEM((parts, n, tok, size), BF16),
+            pltpu.VMEM((parts, n, tok, size), BF16),
+            pltpu.VMEM((rows, LANES), F32),
+            pltpu.VMEM((rows, rows), BF16),
+            pltpu.VMEM((rows, rows), BF16),
+            pltpu.VMEM((8 * chunks, rows), BF16),
+            pltpu.VMEM((CHUNK, rows), BF16),
+            pltpu.VMEM((n, tok), F32),
+            pltpu.VMEM((PAD + rows, state2), F32),
+            pltpu.VMEM((PAD + rows, size), F32),
+            pltpu.VMEM((rows, 2 * CHUNK), BF16),
+            pltpu.VMEM((rows, CHUNK), BF16),
+            pltpu.VMEM((parts, rows, size), F32),
+            pltpu.VMEM((parts, rows, size), F32),
+            pltpu.VMEM((4, 8 * chunks, CHUNK), F32),
+            pltpu.VMEM((rows, size), BF16),
+            pltpu.VMEM((state2 // 2, size), F32),
+            dma((6,)),
+            dma((n,)),
+            dma((n,)),
+            dma((n // plane,)),
+            dma((n,)),
+            dma((n // plane, 3)),
+            dma((parts, n)),
+            dma((parts, n)),
+            dma((2 * parts,)),
+            dma((parts, n)),
+            dma((parts, n)),
+        ],
+        compiler_params=pltpu.CompilerParams(
+            vmem_limit_bytes=48 * 1024 * 1024, collective_id=1, has_side_effects=True
+        ),
+    )(doc_lengths, rate, skip, clip_level, x_rows, bc_rows, step.T, route.T, conv_weight, bias)
+
+
+def fits_fast(n, x_shape, heads, state2):
+    width = x_shape[1] // n
+    owned = heads // n
+    return (
+        n % 8 == 0 and n * x_shape[0] <= 2048 and x_shape[0] == LANES and width % LANES == 0 and state2 == 2 * CHUNK
+        and owned <= 8 and owned % (width // LANES) == 0 and 8 * n * LANES // CHUNK <= CHUNK
+    )
+
+
 def solution(mesh):
     placed = (
         P(("groups", "seq"), None),
@@ -462,8 +930,14 @@
         P(),
         P(),
     )
+
+    def run(*arrays):
+        x_rows, bc_rows, step = arrays[:3]
+        fast = fits_fast(lax.axis_size("seq"), x_rows.shape, step.shape[1], bc_rows.shape[1])
+        return (fast_device if fast else per_device)(*arrays)
+
     return jax.shard_map(
-        per_device,
+        run,
         mesh=mesh,
         in_specs=placed,
         out_specs=P(("groups", "seq"), None),

time: 80.6 us -> 76.9 us (0.954)
  Pallas kernels: 73.7 us -> 69.3 us
  other arithmetic: 1.42 us -> 0 us
  local copies, waits for them, and re-layouts: 4.67 us -> 6.06 us
    pallas_call x1, Pallas kernels: 73.7 us -> 69.3 us  [fast_device(): pl.pallas_call(functools.partial(fast_kernel, owned, parts, plane), out_s...]
    unnamed x4 -> x21, local copies, waits for them, and re-layouts: 3.12 us -> 6.06 us
    broadcast_in_dim x2 -> x0, local copies, waits for them, and re-layouts: 1.34 us -> none  [the longest x1 1.34 us: per_device(): conv_bias[None, :]]
where the time goes in v1:
time: 76.9 us; the launch traced here: 75.4 us
  Pallas kernels  69.3 us (90%)
  local copies, waits for them, and re-layouts  6.06 us (8%)
    pallas_call x1, Pallas kernels, fast_device(): pl.pallas_call(functools.partial(fast_kernel, owned, parts, plane), out_s...  69.3 us
    unnamed x21, local copies, waits for them, and re-layouts  6.06 us

profile of v1, /device:TPU:9, one launch (start us, length us, event | category | flops | bytes accessed | tf_op | source)
XLA Modules:
  0.0 75.4 jit_solution(468996553928430832)
XLA Ops:
  0.0 0.0 copy-start.8
  0.0 0.0 copy-start.9
  0.0 0.0 copy-start.5
  0.0 0.0 copy-start.6
  0.0 0.0 copy-start.7
  0.0 0.6 copy-done.8
  0.7 0.0 copy-done.9
  0.7 0.0 copy-done.5
  0.7 0.0 copy-done.6
  0.7 0.0 copy-done.7
  0.7 0.0 copy-start
  0.7 1.2 %copy-done = bf16[128,4096]{1,0:T(8,128)(2,1)S(1)} copy-done((bf16[128,4096]{1,0:T(8,128)(2,1)S(1)}, bf16[128,4096]{1,0:T(8,128)(2,1)}, u32[]{:S(2)}) %copy-start) | copy-done | bytes 1048600
  1.9 0.0 copy-start.1
  1.9 0.9 %copy-done.1 = f32[4,4352]{1,0:T(4,128)S(1)} copy-done((f32[4,4352]{1,0:T(4,128)S(1)}, f32[4,4352]{1,0:T(4,128)}, u32[]{:S(2)}) %copy-start.1) | copy-done | bytes 69656
  2.8 0.0 copy-start.2
  2.8 0.8 %copy-done.2 = bf16[128,256]{1,0:T(8,128)(2,1)S(1)} copy-done((bf16[128,256]{1,0:T(8,128)(2,1)S(1)}, bf16[128,256]{1,0:T(8,128)(2,1)}, u32[]{:S(2)}) %copy-start.2) | copy-done | bytes 65560
  3.7 0.0 copy-start.3
  3.7 0.7 copy-done.3
  4.4 0.0 copy-start.4
  4.4 0.7 copy-done.4
  5.1 69.3 %shard_map.100 = bf16[128,4096]{1,0:T(8,128)(2,1)S(1)} custom-call(s32[8]{0:T(128)S(1)} %copy-done.5, f32[64]{0:T(128)S(1)} %copy-done.6, f32[64]{0:T(128)S(1)} %copy-done.7, f32[64]{0:T(128)S(1)} %copy-done.8, bf16[128,4096]{1,0:T(8,128)(2,1)S(1)} %copy-done, bf16[128,256]{1,0:T(8,128)(2,1)S(1)} %copy-done.2, bf16[64,128]{1,0:T(8,128)(2,1)S(1)} %bitcast.4, ...), custom_call_target="tpu_custom_call" | custom-call | tf_op jit(solution)/shard_map/pallas_call | solution.py:862
  74.4 1.0 %copy.12 = bf16[128,4096]{1,0:T(8,128)(2,1)} copy(bf16[128,4096]{1,0:T(8,128)(2,1)S(1)} %shard_map.100) | data formatting | bytes 2097152
Async XLA Ops:
  0.0 0.7 copy-start.8
  0.0 0.7 copy-start.9
  0.0 0.7 copy-start.5
  0.0 0.7 copy-start.6
  0.0 0.7 copy-start.7
  0.7 1.2 %copy-start = (bf16[128,4096]{1,0:T(8,128)(2,1)S(1)}, bf16[128,4096]{1,0:T(8,128)(2,1)}, u32[]{:S(2)}) copy-start(bf16[128,4096]{1,0:T(8,128)(2,1)} %x_ref.1) | copy-start | bytes 3145732
  1.9 0.9 %copy-start.1 = (f32[4,4352]{1,0:T(4,128)S(1)}, f32[4,4352]{1,0:T(4,128)}, u32[]{:S(2)}) copy-start(f32[4,4352]{1,0:T(4,128)} %weight_ref.1) | copy-start | bytes 208900
  2.8 0.8 %copy-start.2 = (bf16[128,256]{1,0:T(8,128)(2,1)S(1)}, bf16[128,256]{1,0:T(8,128)(2,1)}, u32[]{:S(2)}) copy-start(bf16[128,256]{1,0:T(8,128)(2,1)} %bc_ref.1) | copy-start | bytes 196612
  3.7 0.7 copy-start.3
  4.4 0.7 copy-start.4

commit v2 on v1

--- a/solution.py
+++ b/solution.py
@@ -467,7 +467,7 @@
 def fast_kernel(
     owned, parts, plane, docs_ref, rates, skips, clips, x_ref, bc_ref, step_ref, route_ref, weight_ref, bias_ref, out_ref,
     step_v, route_v, x_taps, bc_taps, bias_v, small_out, small_all, bc_all, x_all, sent, off_ref,
-    sorter, unsorter, dt_left, dt_right, places, ub, ux, lhs, b_flip, rise, fall, by_chunk, ys, state,
+    sorter, unsorter, columns, dt_left, dt_right, places, ub, ux, lhs, b_flip, rise, fall, by_chunk, ys, state,
     load_sem, small_send, small_recv, gate_send, gate_recv, plane_send, x_send, x_recv, own_sem, out_send, out_recv,
 ):
     n, tok, state2 = bc_all.shape
@@ -550,12 +550,31 @@
         peer = across if hop == 0 else sibling
         return remote(bc_all.at[owner], bc_all.at[owner], plane_send.at[k, hop], gate_recv.at[owner], peer)
 
-    def x_copy(part, k):
-        peer = lax.rem(me + k, n)
-        return remote(tile(x_ref, part, peer), x_all.at[part, me], x_send.at[part, k], x_recv.at[part, me], peer)
+    def x_copy(part, peer):
+        return remote(tile(x_ref, part, peer), x_all.at[part, me], x_send.at[part, peer], x_recv.at[part, me], peer)
+
+    planes = n // plane
+    half = planes // 2
+    mine = me // plane
+
+    def plane_at(i):
+        turn = lax.rem(i, half)
+        side = lax.rem(mine // half + 1 + i // half, 2)
+        return side * half + lax.rem(lax.rem(mine, half) + turn + i // half, half)
 
     def own_copy(part):
         return pltpu.make_async_copy(tile(x_ref, part, me), x_all.at[part, me], own_sem.at[part])
+
+    def start_x(part):
+        def to_plane(i):
+            for j in range(plane):
+                peer = plane_at(i) * plane + lax.rem(inside + 1 + j, plane)
+
+                @pl.when(peer != me)
+                def _():
+                    x_copy(part, peer).start()
+
+        every(planes, to_plane)
 
     every(n, lambda k: small_copy(k).start(), 1)
     every(n // plane, lambda k: far(k).start(), 1)
@@ -563,8 +582,6 @@
     relay(0, 1).start()
     for part in range(parts):
         own_copy(part).start()
-    for part in range(parts):
-        every(n, lambda k: x_copy(part, k).start(), 1)
 
     starts, total = [], jnp.int32(0)
     for k in range(docs_ref.shape[0]):
@@ -577,19 +594,19 @@
             begin = jnp.where(at >= start, start, begin)
         return begin
 
-    def forward(k):
-        landed(bc_all, gate_recv, lax.rem(me + k * plane, n)).wait_recv()
-        relay(k, 0).start()
-        relay(k, 1).start()
-
-    every(n // plane, forward, 1)
+    low, high = iota((CHUNK, CHUNK), 0), iota((CHUNK, CHUNK), 1)
+
+    def make_off(c):
+        base = pl.multiple_of(c * CHUNK, CHUNK)
+        at = low + base
+        off_ref[pl.ds(base, CHUNK), :] = (at - begins(at)).astype(F32)
+
+    every(chunks, make_off)
 
     def small_landed(k):
         landed(small_all, small_recv, lax.rem(me + k, n)).wait_recv()
 
     every(n, small_landed, 1)
-
-    low, high = iota((CHUNK, CHUNK), 0), iota((CHUNK, CHUNK), 1)
 
     def find_places():
         number = iota((n, tok), 0).astype(F32)
@@ -609,9 +626,11 @@
         base = jnp.zeros((n, tok), F32)
         for d in range(n - 1):
             base = base + jnp.where(number > d, before[d : d + 1, :], 0.0)
+        all_places = []
         for i in range(n):
             place = jnp.sum(named[i] * (ranks[i] + base), axis=0, keepdims=True)
             places[i : i + 1, :] = place
+            all_places.append(place)
             coarse = jnp.floor(place * (1.0 / CHUNK))
             fine = place - coarse * CHUNK
             lanes = slice(i * tok, (i + 1) * tok)
@@ -636,18 +655,20 @@
 
     every(rows // SUB, make_sorter)
 
+    def forward(k):
+        landed(bc_all, gate_recv, lax.rem(me + k * plane, n)).wait_recv()
+        relay(k, 0).start()
+        relay(k, 1).start()
+
+    every(n // plane, forward, 1)
+    start_x(0)
+
     def crossed(k):
         landed(bc_all, gate_recv, lax.rem(across + k * plane, n)).wait_recv()
         relay(k, 2).start()
 
     every(n // plane, crossed)
 
-    def make_off(c):
-        base = pl.multiple_of(c * CHUNK, CHUNK)
-        at = low + base
-        off_ref[pl.ds(base, CHUNK), :] = (at - begins(at)).astype(F32)
-
-    every(chunks, make_off)
 
     def decays():
         dts = dot_nt(dt_left[...], dt_right[...])
@@ -684,16 +705,38 @@
             out = jnp.where(head == h, jnp.broadcast_to(columns[:, at : at + 1], (CHUNK, size)), out)
         return out
 
-    def expand(c):
-        base = pl.multiple_of(c * CHUNK, CHUNK)
-        at8 = pl.ds(pl.multiple_of(c * 8, 8), 8)
-        rest = jnp.zeros((CHUNK - 16, CHUNK), F32)
-        columns = jnp.concatenate([by_chunk[0, at8, :], by_chunk[1, at8, :], rest], axis=0).T
-        for part in range(parts):
-            rise[part, pl.ds(base, CHUNK), :] = spread(columns, part)
-            fall[part, pl.ds(base, CHUNK), :] = spread(columns[:, 8:], part)
-
-    every(chunks // 4, lambda c: [expand(4 * c + i) for i in range(4)])
+    def expand():
+        pair = by_chunk[0].reshape(chunks, 8, CHUNK)[:, :4], by_chunk[1].reshape(chunks, 8, CHUNK)[:, :4]
+        turned = jnp.concatenate(pair, axis=1).reshape(8 * chunks, CHUNK).T
+        for c in range(chunks):
+            at = slice(c * CHUNK, (c + 1) * CHUNK)
+            for part in range(parts):
+                rise[part, at, :] = spread(turned[:, 8 * c :], part)
+                fall[part, at, :] = spread(turned[:, 8 * c + 4 :], part)
+
+    expand()
+
+    lane16 = [(iota((tok, LANES), 1) + j * LANES).astype(F32).astype(BF16) for j in range(SUB // LANES)]
+    flipped = jnp.concatenate([places[...], jnp.zeros((tok - n, tok), F32)], axis=0).T
+    flipped_coarse = jnp.floor(flipped * (1.0 / SUB))
+    flipped_fine = flipped - flipped_coarse * SUB
+
+    def make_columns():
+        for i in range(n):
+            at = slice(i * tok, (i + 1) * tok)
+            columns[0, at, :] = jnp.broadcast_to(flipped_coarse[:, i : i + 1], (tok, LANES)).astype(BF16)
+            columns[1, at, :] = jnp.broadcast_to(flipped_fine[:, i : i + 1], (tok, LANES)).astype(BF16)
+
+    def make_unsorter(i):
+        at = pl.ds(pl.multiple_of(i * tok, tok), tok)
+        coarse, fine = columns[0, at, :], columns[1, at, :]
+        for b in range(rows // SUB):
+            rel = jnp.where(coarse == jnp.full((), b, BF16), fine, -one)
+            for j in range(SUB // LANES):
+                unsorter[at, b * SUB + j * LANES : b * SUB + (j + 1) * LANES] = jnp.where(lane16[j] == rel, one, none)
+
+    make_columns()
+    every(n, make_unsorter)
 
     def rest(k):
         for hop in (0, 2):
@@ -702,11 +745,13 @@
 
     every(n // plane, rest)
 
+    start_x(1)
+
     for load in loads[3:]:
         load.wait()
     ub[0:PAD, :] = jnp.zeros((PAD, state2), F32)
     ux[0:PAD, :] = jnp.zeros((PAD, size), F32)
-    block = 512
+    block = plane * tok
 
     def gather(b):
         first = pl.multiple_of(b * block, block)
@@ -736,19 +781,6 @@
         b_flip[pl.ds(base, CHUNK), :] = jnp.where(runs_out, b_mat.astype(F32).T, 0.0).astype(BF16)
 
     every(chunks // 4, lambda c: [shared(4 * c + i) for i in range(4)])
-
-    col16 = iota((tok, SUB), 1).astype(F32).astype(BF16)
-    flipped = jnp.concatenate([places[...], jnp.zeros((tok - n, tok), F32)], axis=0).T
-
-    def make_unsorter(b):
-        first = lax.convert_element_type(b * SUB, F32)
-        for i in range(n):
-            rel = jnp.broadcast_to(flipped[:, i : i + 1], (tok, tok)) - first
-            rel = jnp.where((rel >= 0.0) & (rel < SUB), rel, -1.0).astype(BF16)
-            hit = jnp.where(col16 == jnp.concatenate([rel] * (SUB // tok), axis=1), one, none)
-            unsorter[i * tok : (i + 1) * tok, pl.ds(pl.multiple_of(b * SUB, SUB), SUB)] = hit
-
-    every(rows // SUB, make_unsorter)
 
     def out_copy(part, owner):
         return remote(
@@ -806,7 +838,7 @@
         every(chunks // 4, lambda c: [chunk(4 * c + i) for i in range(4)])
 
         def scatter(i):
-            b = lax.rem(me * tok // block + 1 + i, rows // block)
+            b = plane_at(i)
             first = pl.multiple_of(b * block, block)
             back = dot(unsorter[pl.ds(first, block), :], ys[...]).astype(BF16)
             for j in range(block // tok):
@@ -826,7 +858,7 @@
             slot = tile(out_ref, part, source)
             remote(slot, slot, gate_send.at[0], out_recv.at[part, source], source).wait_recv()
             out_copy(part, source).wait_send()
-            x_copy(part, k).wait_send()
+            x_copy(part, source).wait_send()
         small_copy(k).wait_send()
 
     every(n, finish, 1)
@@ -878,6 +910,7 @@
             pltpu.VMEM((rows, LANES), F32),
             pltpu.VMEM((rows, rows), BF16),
             pltpu.VMEM((rows, rows), BF16),
+            pltpu.VMEM((2, rows, LANES), BF16),
             pltpu.VMEM((8 * chunks, rows), BF16),
             pltpu.VMEM((CHUNK, rows), BF16),
             pltpu.VMEM((n, tok), F32),
@@ -905,7 +938,9 @@
         compiler_params=pltpu.CompilerParams(
             vmem_limit_bytes=48 * 1024 * 1024, collective_id=1, has_side_effects=True
         ),
-    )(doc_lengths, rate, skip, clip_level, x_rows, bc_rows, step.T, route.T, conv_weight, bias)
+    )(*[pltpu.with_memory_space_constraint(a, pltpu.HBM) for a in (
+        doc_lengths, rate, skip, clip_level, x_rows, bc_rows, step.T, route.T, conv_weight, bias
+    )])
 
 
 def fits_fast(n, x_shape, heads, state2):
@@ -913,7 +948,7 @@
     owned = heads // n
     return (
         n % 8 == 0 and n * x_shape[0] <= 2048 and x_shape[0] == LANES and width % LANES == 0 and state2 == 2 * CHUNK
-        and owned <= 8 and owned % (width // LANES) == 0 and 8 * n * LANES // CHUNK <= CHUNK
+        and owned == 4 and owned % (width // LANES) == 0 and 8 * n * LANES // CHUNK <= CHUNK
     )
 
 

time: 76.9 us -> 65.2 us (0.85)
  the two profiles are of different devices: /device:TPU:9 before, /device:TPU:23 now
where the time goes in v2:
time: 65.2 us; the launch traced here: 65 us
  Pallas kernels  64 us (98%)
  local copies, waits for them, and re-layouts  0.97 us (1%)
    pallas_call x1, Pallas kernels, fast_device(): pl.pallas_call(functools.partial(fast_kernel, owned, parts, plane), out_s...  64 us

profile of v2, /device:TPU:23, one launch (start us, length us, event | category | flops | bytes accessed | tf_op | source)
XLA Modules:
  0.0 65.0 jit_solution(4452286986954835420)
XLA Ops:
  0.0 64.0 %shard_map.100 = bf16[128,4096]{1,0:T(8,128)(2,1)S(1)} custom-call(s32[8]{0:T(128)} %docs_ref.1, f32[64]{0:T(128)} %rates.1, f32[64]{0:T(128)} %skips.1, f32[64]{0:T(128)} %clips.1, bf16[128,4096]{1,0:T(8,128)(2,1)} %x_ref.1, bf16[128,256]{1,0:T(8,128)(2,1)} %bc_ref.1, bf16[64,128]{1,0:T(8,128)(2,1)} %bitcast.4, s32[1,128]{1,0:T(1,128)} %bitcast.5, ...), custom_call_target="tpu_custom_call" | custom-call | tf_op jit(solution)/shard_map/pallas_call | solution.py:894
  64.0 1.0 %copy.12 = bf16[128,4096]{1,0:T(8,128)(2,1)} copy(bf16[128,4096]{1,0:T(8,128)(2,1)S(1)} %shard_map.100) | data formatting | bytes 2097152

commit v3 on v2

--- a/solution.py
+++ b/solution.py
@@ -12,6 +12,7 @@
 CHUNK = 128
 LANES = 128
 PAD = 8
+SCHEDULE = {7:[(0,0)],1:[(0,1)],2:[(0,2),(0,3)],3:[(1,0),(1,1),(1,2),(1,3)]}
 OUT_SPEC = pl.BlockSpec(memory_space=pl.ANY)
 
 
@@ -531,9 +532,13 @@
 
     pl.semaphore_wait(barrier, n - 1)
 
-    def far(k):
-        peer = lax.rem(me + k * plane, n)
-        return remote(bc_all.at[me], bc_all.at[me], gate_send.at[k], gate_recv.at[me], peer)
+    low_plane = lax.rem(me // plane, 2)
+    mate_turn, last_turn = 1 + 2 * low_plane, 3 - 2 * low_plane
+
+    def far(step):
+        owner = lax.rem(me + 2 * plane, n) if step == 2 else me
+        peer = lax.rem(me + (2 if step == 0 else mate_turn) * plane, n)
+        return remote(bc_all.at[owner], bc_all.at[owner], gate_send.at[step], gate_recv.at[owner], peer)
 
     def small_copy(k):
         peer = lax.rem(me + k, n)
@@ -565,21 +570,25 @@
     def own_copy(part):
         return pltpu.make_async_copy(tile(x_ref, part, me), x_all.at[part, me], own_sem.at[part])
 
-    def start_x(part):
-        def to_plane(i):
-            for j in range(plane):
-                peer = plane_at(i) * plane + lax.rem(inside + 1 + j, plane)
+    def start_at(moment):
+        for part, turn in SCHEDULE.get(moment, ()):
+            first = plane_at(jnp.int32(turn)) * plane
+
+            def to_peer(j, part=part, first=first):
+                peer = first + lax.rem(inside + 1 + j, plane)
 
                 @pl.when(peer != me)
                 def _():
                     x_copy(part, peer).start()
 
-        every(planes, to_plane)
+            every(plane, to_peer)
 
     every(n, lambda k: small_copy(k).start(), 1)
-    every(n // plane, lambda k: far(k).start(), 1)
+    far(0).start()
+    far(1).start()
     relay(0, 0).start()
     relay(0, 1).start()
+    start_at(0)
     for part in range(parts):
         own_copy(part).start()
 
@@ -641,6 +650,7 @@
 
     find_places()
 
+    start_at(6)
     row16 = iota((SUB, tok), 0).astype(F32).astype(BF16)
     one, none = jnp.ones((), BF16), jnp.zeros((), BF16)
 
@@ -655,20 +665,28 @@
 
     every(rows // SUB, make_sorter)
 
+    start_at(8)
     def forward(k):
         landed(bc_all, gate_recv, lax.rem(me + k * plane, n)).wait_recv()
+        if isinstance(k, int):
+            far(2).start()
         relay(k, 0).start()
         relay(k, 1).start()
 
-    every(n // plane, forward, 1)
-    start_x(0)
+    forward(2)
+    forward(mate_turn)
+    start_at(7)
+    forward(last_turn)
+    start_at(1)
 
     def crossed(k):
         landed(bc_all, gate_recv, lax.rem(across + k * plane, n)).wait_recv()
         relay(k, 2).start()
 
-    every(n // plane, crossed)
-
+    for k in (0, 2, mate_turn, last_turn):
+        crossed(k)
+
+    start_at(2)
 
     def decays():
         dts = dot_nt(dt_left[...], dt_right[...])
@@ -735,6 +753,7 @@
             for j in range(SUB // LANES):
                 unsorter[at, b * SUB + j * LANES : b * SUB + (j + 1) * LANES] = jnp.where(lane16[j] == rel, one, none)
 
+    start_at(9)
     make_columns()
     every(n, make_unsorter)
 
@@ -745,7 +764,7 @@
 
     every(n // plane, rest)
 
-    start_x(1)
+    start_at(3)
 
     for load in loads[3:]:
         load.wait()
@@ -759,6 +778,7 @@
         ub[pl.ds(pl.multiple_of(first + PAD, PAD), block), :] = here
 
     every(rows // block, gather)
+    start_at(4)
 
     gap = low - high
 
@@ -781,6 +801,7 @@
         b_flip[pl.ds(base, CHUNK), :] = jnp.where(runs_out, b_mat.astype(F32).T, 0.0).astype(BF16)
 
     every(chunks // 4, lambda c: [shared(4 * c + i) for i in range(4)])
+    start_at(5)
 
     def out_copy(part, owner):
         return remote(
@@ -870,7 +891,8 @@
             relay(k, hop).wait_send()
 
     every(n // plane, finish_aux)
-    every(n // plane, lambda k: far(k).wait_send(), 1)
+    for step in range(3):
+        far(step).wait_send()
 
 
 def fast_device(
@@ -947,7 +969,7 @@
     width = x_shape[1] // n
     owned = heads // n
     return (
-        n % 8 == 0 and n * x_shape[0] <= 2048 and x_shape[0] == LANES and width % LANES == 0 and state2 == 2 * CHUNK
+        n == 16 and n * x_shape[0] <= 2048 and x_shape[0] == LANES and width % LANES == 0 and state2 == 2 * CHUNK
         and owned == 4 and owned % (width // LANES) == 0 and 8 * n * LANES // CHUNK <= CHUNK
     )
 

time: 65.2 us -> 63.5 us (0.974)
  the two profiles are of different devices: /device:TPU:23 before, /device:TPU:9 now
where the time goes in v3:
time: 63.5 us; the launch traced here: 62.6 us
  Pallas kernels  61.6 us (97%)
  local copies, waits for them, and re-layouts  0.97 us (2%)
    pallas_call x1, Pallas kernels, fast_device(): pl.pallas_call(functools.partial(fast_kernel, owned, parts, plane), out_s...  61.6 us

profile of v3, /device:TPU:9, one launch (start us, length us, event | category | flops | bytes accessed | tf_op | source)
XLA Modules:
  0.0 62.6 jit_solution(16079987881342815025)
XLA Ops:
  0.0 61.6 %shard_map.100 = bf16[128,4096]{1,0:T(8,128)(2,1)S(1)} custom-call(s32[8]{0:T(128)} %docs_ref.1, f32[64]{0:T(128)} %rates.1, f32[64]{0:T(128)} %skips.1, f32[64]{0:T(128)} %clips.1, bf16[128,4096]{1,0:T(8,128)(2,1)} %x_ref.1, bf16[128,256]{1,0:T(8,128)(2,1)} %bc_ref.1, bf16[64,128]{1,0:T(8,128)(2,1)} %bitcast.4, s32[1,128]{1,0:T(1,128)} %bitcast.5, ...), custom_call_target="tpu_custom_call" | custom-call | tf_op jit(solution)/shard_map/pallas_call | solution.py:916
  61.7 1.0 %copy.12 = bf16[128,4096]{1,0:T(8,128)(2,1)} copy(bf16[128,4096]{1,0:T(8,128)(2,1)S(1)} %shard_map.100) | data formatting | bytes 2097152

commit v4 on v3

--- a/solution.py
+++ b/solution.py
@@ -12,7 +12,13 @@
 CHUNK = 128
 LANES = 128
 PAD = 8
-SCHEDULE = {7:[(0,0)],1:[(0,1)],2:[(0,2),(0,3)],3:[(1,0),(1,1),(1,2),(1,3)]}
+SCHEDULE = {
+    0: ((0, 0, 0, 2),),
+    7: ((0, 0, 2, 4),),
+    1: ((0, 1),),
+    2: ((0, 2), (0, 3)),
+    3: ((1, 0), (1, 1), (1, 2), (1, 3)),
+}
 OUT_SPEC = pl.BlockSpec(memory_space=pl.ANY)
 
 
@@ -571,7 +577,8 @@
         return pltpu.make_async_copy(tile(x_ref, part, me), x_all.at[part, me], own_sem.at[part])
 
     def start_at(moment):
-        for part, turn in SCHEDULE.get(moment, ()):
+        for part, turn, *span in SCHEDULE.get(moment, ()):
+            begin, end = span or (0, plane)
             first = plane_at(jnp.int32(turn)) * plane
 
             def to_peer(j, part=part, first=first):
@@ -581,7 +588,7 @@
                 def _():
                     x_copy(part, peer).start()
 
-            every(plane, to_peer)
+            every(end, to_peer, begin)
 
     every(n, lambda k: small_copy(k).start(), 1)
     far(0).start()
@@ -679,15 +686,6 @@
     forward(last_turn)
     start_at(1)
 
-    def crossed(k):
-        landed(bc_all, gate_recv, lax.rem(across + k * plane, n)).wait_recv()
-        relay(k, 2).start()
-
-    for k in (0, 2, mate_turn, last_turn):
-        crossed(k)
-
-    start_at(2)
-
     def decays():
         dts = dot_nt(dt_left[...], dt_right[...])
         lane = iota((8, CHUNK), 1)
@@ -723,16 +721,38 @@
             out = jnp.where(head == h, jnp.broadcast_to(columns[:, at : at + 1], (CHUNK, size)), out)
         return out
 
-    def expand():
+    def expand(part):
         pair = by_chunk[0].reshape(chunks, 8, CHUNK)[:, :4], by_chunk[1].reshape(chunks, 8, CHUNK)[:, :4]
         turned = jnp.concatenate(pair, axis=1).reshape(8 * chunks, CHUNK).T
         for c in range(chunks):
             at = slice(c * CHUNK, (c + 1) * CHUNK)
-            for part in range(parts):
-                rise[part, at, :] = spread(turned[:, 8 * c :], part)
-                fall[part, at, :] = spread(turned[:, 8 * c + 4 :], part)
-
-    expand()
+            rise[part, at, :] = spread(turned[:, 8 * c :], part)
+            fall[part, at, :] = spread(turned[:, 8 * c + 4 :], part)
+
+    expand(0)
+
+    def crossed(k):
+        landed(bc_all, gate_recv, lax.rem(across + k * plane, n)).wait_recv()
+        relay(k, 2).start()
+
+    for k in (0, 2, mate_turn, last_turn):
+        crossed(k)
+
+    start_at(2)
+
+    block = plane * tok
+    core = lax.rem(me, 2)
+    ub[0:PAD, :] = jnp.zeros((PAD, state2), F32)
+
+    def gather(b, side):
+        first = pl.multiple_of(b * block, block)
+        owners = [2 * i + side for i in range(n // 2)]
+        lefts = [sorter[pl.ds(first, block), pl.ds(pl.multiple_of(o * tok, tok), tok)] for o in owners]
+        here = dot(jnp.concatenate(lefts, axis=1), jnp.concatenate([bc_all[o] for o in owners], axis=0))
+        at = pl.ds(pl.multiple_of(first + PAD, PAD), block)
+        ub[at, :] = here if side is core else ub[at, :] + here
+
+    every(rows // block, lambda b: gather(b, core))
 
     lane16 = [(iota((tok, LANES), 1) + j * LANES).astype(F32).astype(BF16) for j in range(SUB // LANES)]
     flipped = jnp.concatenate([places[...], jnp.zeros((tok - n, tok), F32)], axis=0).T
@@ -755,7 +775,6 @@
 
     start_at(9)
     make_columns()
-    every(n, make_unsorter)
 
     def rest(k):
         for hop in (0, 2):
@@ -768,16 +787,8 @@
 
     for load in loads[3:]:
         load.wait()
-    ub[0:PAD, :] = jnp.zeros((PAD, state2), F32)
     ux[0:PAD, :] = jnp.zeros((PAD, size), F32)
-    block = plane * tok
-
-    def gather(b):
-        first = pl.multiple_of(b * block, block)
-        here = dot(sorter[pl.ds(first, block), :], bc_all[...].reshape(rows, state2))
-        ub[pl.ds(pl.multiple_of(first + PAD, PAD), block), :] = here
-
-    every(rows // block, gather)
+    every(rows // block, lambda b: gather(b, 1 - core))
     start_at(4)
 
     gap = low - high
@@ -826,6 +837,8 @@
             slot = x_all.at[part, source]
             remote(slot, slot, gate_send.at[0], x_recv.at[part, source], source).wait_recv()
 
+        if part > 0:
+            expand(part)
         own_copy(part).wait()
         every(n, x_landed, 1)
 
@@ -861,6 +874,8 @@
         def scatter(i):
             b = plane_at(i)
             first = pl.multiple_of(b * block, block)
+            if part == 0:
+                every(plane, lambda j: make_unsorter(b * plane + j))
             back = dot(unsorter[pl.ds(first, block), :], ys[...]).astype(BF16)
             for j in range(block // tok):
                 owner = b * (block // tok) + j

time: 63.5 us -> 59.8 us (0.942); the launches traced: 62.6 us -> 59.6 us
  Pallas kernels: 61.6 us -> 58.6 us
    pallas_call x1, Pallas kernels: 61.6 us -> 58.6 us  [fast_device(): pl.pallas_call(functools.partial(fast_kernel, owned, parts, plane), out_s...]
where the time goes in v4:
time: 59.8 us; the launch traced here: 59.6 us
  Pallas kernels  58.6 us (98%)
  local copies, waits for them, and re-layouts  0.97 us (2%)
    pallas_call x1, Pallas kernels, fast_device(): pl.pallas_call(functools.partial(fast_kernel, owned, parts, plane), out_s...  58.6 us

profile of v4, /device:TPU:9, one launch (start us, length us, event | category | flops | bytes accessed | tf_op | source)
XLA Modules:
  0.0 59.6 jit_solution(13257920936649909397)
XLA Ops:
  0.0 58.6 %shard_map.100 = bf16[128,4096]{1,0:T(8,128)(2,1)S(1)} custom-call(s32[8]{0:T(128)} %docs_ref.1, f32[64]{0:T(128)} %rates.1, f32[64]{0:T(128)} %skips.1, f32[64]{0:T(128)} %clips.1, bf16[128,4096]{1,0:T(8,128)(2,1)} %x_ref.1, bf16[128,256]{1,0:T(8,128)(2,1)} %bc_ref.1, bf16[64,128]{1,0:T(8,128)(2,1)} %bitcast.4, s32[1,128]{1,0:T(1,128)} %bitcast.5, ...), custom_call_target="tpu_custom_call" | custom-call | tf_op jit(solution)/shard_map/pallas_call | solution.py:931
  58.6 1.0 %copy.12 = bf16[128,4096]{1,0:T(8,128)(2,1)} copy(bf16[128,4096]{1,0:T(8,128)(2,1)S(1)} %shard_map.100) | data formatting | bytes 2097152

commit v5 on v4

--- a/solution.py
+++ b/solution.py
@@ -12,13 +12,7 @@
 CHUNK = 128
 LANES = 128
 PAD = 8
-SCHEDULE = {
-    0: ((0, 0, 0, 2),),
-    7: ((0, 0, 2, 4),),
-    1: ((0, 1),),
-    2: ((0, 2), (0, 3)),
-    3: ((1, 0), (1, 1), (1, 2), (1, 3)),
-}
+SCHEDULE = {0:[(0,0,0,2)],7:[(0,0,2,4)],1:[(0,1)],2:[(0,2),(0,3)],3:[(1,0),(1,1),(1,2),(1,3)]}
 OUT_SPEC = pl.BlockSpec(memory_space=pl.ANY)
 
 
@@ -510,8 +504,6 @@
             barrier, inc=1, device_id={"seq": lax.rem(me + k, n)}, device_id_type=pl.DeviceIdType.MESH
         )
 
-    every(n, greet, 1)
-
     own = pl.ds(pl.multiple_of(me * width, width), width)
     shared_at = weight_ref.shape[1] - state2
     loads = [
@@ -522,7 +514,10 @@
         pltpu.make_async_copy(weight_ref.at[:, shared_at:], bc_taps, load_sem.at[4]),
         pltpu.make_async_copy(bias_ref, bias_v, load_sem.at[5]),
     ]
-    for load in loads:
+    for load in loads[:3]:
+        load.start()
+    every(n, greet, 1)
+    for load in loads[3:]:
         load.start()
 
     loads[1].wait()
@@ -830,6 +825,14 @@
             out = jnp.where(lane_head == h, values[h], out)
         return out
 
+    def finish_aux():
+        every(n, lambda k: small_copy(k).wait_send(), 1)
+        for step in range(3):
+            far(step).wait_send()
+        for k in range(n // plane):
+            for hop in range(3):
+                relay(k, hop).wait_send()
+
     for part in range(parts):
 
         def x_landed(k):
@@ -839,6 +842,10 @@
 
         if part > 0:
             expand(part)
+        if part == 1:
+            finish_aux()
+        if part > 0:
+            every(n, lambda k: x_copy(part - 1, lax.rem(me + k, n)).wait_send(), 1)
         own_copy(part).wait()
         every(n, x_landed, 1)
 
@@ -888,26 +895,26 @@
         every(rows // block, scatter)
         own_out(part).start()
 
-    def finish(k):
-        source = lax.rem(me + k, n)
-        for part in range(parts):
-            slot = tile(out_ref, part, source)
-            remote(slot, slot, gate_send.at[0], out_recv.at[part, source], source).wait_recv()
-            out_copy(part, source).wait_send()
-            x_copy(part, source).wait_send()
-        small_copy(k).wait_send()
-
-    every(n, finish, 1)
+    def x_sent(part):
+        every(n, lambda k: x_copy(part, lax.rem(me + k, n)).wait_send(), 1)
+
+    def finish(part):
+        def from_plane(i):
+            for j in range(plane):
+                source = plane_at(i) * plane + lax.rem(inside + 1 + j, plane)
+
+                @pl.when(source != me)
+                def _():
+                    slot = tile(out_ref, part, source)
+                    out_copy(part, source).wait_send()
+                    remote(slot, slot, gate_send.at[0], out_recv.at[part, source], source).wait_recv()
+
+        every(planes, from_plane)
+
+    x_sent(parts - 1)
     for part in range(parts):
         own_out(part).wait()
-
-    def finish_aux(k):
-        for hop in range(3):
-            relay(k, hop).wait_send()
-
-    every(n // plane, finish_aux)
-    for step in range(3):
-        far(step).wait_send()
+        finish(part)
 
 
 def fast_device(
@@ -985,7 +992,7 @@
     owned = heads // n
     return (
         n == 16 and n * x_shape[0] <= 2048 and x_shape[0] == LANES and width % LANES == 0 and state2 == 2 * CHUNK
-        and owned == 4 and owned % (width // LANES) == 0 and 8 * n * LANES // CHUNK <= CHUNK
+        and owned == 4 and width // LANES == 2 and 8 * n * LANES // CHUNK <= CHUNK
     )
 
 

time: 59.8 us -> 59.9 us (level)
  no operation moved by 1% of the time
where the time goes in v5:
time: 59.9 us; the launch traced here: 59.4 us
  Pallas kernels  58.5 us (98%)
  local copies, waits for them, and re-layouts  0.97 us (2%)
    pallas_call x1, Pallas kernels, fast_device(): pl.pallas_call(functools.partial(fast_kernel, owned, parts, plane), out_s...  58.5 us

profile of v5, /device:TPU:9, one launch (start us, length us, event | category | flops | bytes accessed | tf_op | source)
XLA Modules:
  0.0 59.4 jit_solution(8298552740452554321)
XLA Ops:
  0.0 58.5 %shard_map.100 = bf16[128,4096]{1,0:T(8,128)(2,1)S(1)} custom-call(s32[8]{0:T(128)} %docs_ref.1, f32[64]{0:T(128)} %rates.1, f32[64]{0:T(128)} %skips.1, f32[64]{0:T(128)} %clips.1, bf16[128,4096]{1,0:T(8,128)(2,1)} %x_ref.1, bf16[128,256]{1,0:T(8,128)(2,1)} %bc_ref.1, bf16[64,128]{1,0:T(8,128)(2,1)} %bitcast.4, s32[1,128]{1,0:T(1,128)} %bitcast.5, ...), custom_call_target="tpu_custom_call" | custom-call | tf_op jit(solution)/shard_map/pallas_call | solution.py:938
  58.5 1.0 %copy.12 = bf16[128,4096]{1,0:T(8,128)(2,1)} copy(bf16[128,4096]{1,0:T(8,128)(2,1)S(1)} %shard_map.100) | data formatting | bytes 2097152

commit v6 on v4

--- a/solution.py
+++ b/solution.py
@@ -592,8 +592,8 @@
 
     every(n, lambda k: small_copy(k).start(), 1)
     far(0).start()
+    relay(0, 0).start()
     far(1).start()
-    relay(0, 0).start()
     relay(0, 1).start()
     start_at(0)
     for part in range(parts):

time: 59.8 us -> 59.8 us (level)
  no operation moved by 1% of the time
where the time goes in v6:
time: 59.8 us; the launch traced here: 59.6 us
  Pallas kernels  58.6 us (98%)
  local copies, waits for them, and re-layouts  0.97 us (2%)
    pallas_call x1, Pallas kernels, fast_device(): pl.pallas_call(functools.partial(fast_kernel, owned, parts, plane), out_s...  58.6 us

profile of v6, /device:TPU:9, one launch (start us, length us, event | category | flops | bytes accessed | tf_op | source)
XLA Modules:
  0.0 59.6 jit_solution(5331509360052961981)
XLA Ops:
  0.0 58.6 %shard_map.100 = bf16[128,4096]{1,0:T(8,128)(2,1)S(1)} custom-call(s32[8]{0:T(128)} %docs_ref.1, f32[64]{0:T(128)} %rates.1, f32[64]{0:T(128)} %skips.1, f32[64]{0:T(128)} %clips.1, bf16[128,4096]{1,0:T(8,128)(2,1)} %x_ref.1, bf16[128,256]{1,0:T(8,128)(2,1)} %bc_ref.1, bf16[64,128]{1,0:T(8,128)(2,1)} %bitcast.4, s32[1,128]{1,0:T(1,128)} %bitcast.5, ...), custom_call_target="tpu_custom_call" | custom-call | tf_op jit(solution)/shard_map/pallas_call | solution.py:931
  58.6 1.0 %copy.12 = bf16[128,4096]{1,0:T(8,128)(2,1)} copy(bf16[128,4096]{1,0:T(8,128)(2,1)S(1)} %shard_map.100) | data formatting | bytes 2097152
